TPU v7x, 32 devices: a whole 2x2x4 slice. The times are simulated.
32 devices in a mesh: win: 2 (over x), chan: 16 (over z, y, core).
Axes of the slice: x: 2, y: 2, z: 4, core: 2. Of those that a mesh axis runs over, the one named last changes fastest.
Arguments:
- spectra: bfloat16 [8, 256, 2, 2048], P('win', 'chan')
- window_gain: float32 [8], P('win'), may hold values from 0.4 to 3
- dead_mask: int32 [8, 256], P('win', 'chan'), may hold values 0 or 1
- order: int32 [256], replicated, may hold values from 0 to 15
Outputs:
- stack: bfloat16 [256, 256, 2, 2048], P(None, 'chan', None, 'win')
- window_weight: float32 [8], P('win')
All inputs are finite; a program needn't handle non-finite values. No bound on the sum of `dead_mask` on one device may be relied on, other than what follows from the above.
Results may differ from a plain program's by a relative error of at most 0.0064.
Values may be sent and summed in bfloat16 or wider, within the bound.
A program may use at most 128 MiB of HBM per device.

v0:
```python
import jax
import jax.numpy as jnp
from jax import lax
from jax.sharding import PartitionSpec as P

ITERS = 2


def solve_stack(src_re, src_im, ch_re, ch_im, cells):
    f32 = jnp.float32
    bf16 = jnp.bfloat16
    corr_form = "ksf,kcf->scf"
    proj_form = "ksf,scf->kcf"
    row_axis = 1
    freq_axis = 1
    cross_axes = (1, 2)
    count = src_re.shape[0]
    a_square = jnp.sum(
        jnp.square(src_re.astype(f32)) + jnp.square(src_im.astype(f32)), axis=row_axis
    )
    b_square = jnp.sum(jnp.square(ch_re.astype(f32)) + jnp.square(ch_im.astype(f32)), axis=row_axis)
    energy = jnp.sum(a_square * b_square, axis=freq_axis)

    def product(form, left, right):
        return jnp.einsum(form, left, right, preferred_element_type=f32)

    def stack_of(weight):
        shaped = weight[:, None, None]
        w_re = (shaped * ch_re.astype(f32)).astype(bf16)
        w_im = (shaped * ch_im.astype(f32)).astype(bf16)
        total = jnp.sum(weight)
        gre = (product(corr_form, src_re, w_re) + product(corr_form, src_im, w_im)) / total
        gim = (product(corr_form, src_re, w_im) - product(corr_form, src_im, w_re)) / total
        return (gre.astype(bf16), gim.astype(bf16))

    weight = jnp.ones((count,), f32)
    for step in range(ITERS):
        gre, gim = stack_of(weight)
        p_re = product(proj_form, src_re, gre) - product(proj_form, src_im, gim)
        p_im = product(proj_form, src_re, gim) + product(proj_form, src_im, gre)
        cross = jnp.sum(ch_re.astype(f32) * p_re + ch_im.astype(f32) * p_im, axis=cross_axes)
        power = jnp.sum(jnp.square(gre.astype(f32)) + jnp.square(gim.astype(f32)))
        partial_misfit = energy - 2.0 * cross + power
        misfit = lax.psum(partial_misfit, ("win", "chan"))
        weight = 1.0 / jnp.sqrt(misfit / cells + 1e-06)
    gre, gim = stack_of(weight)
    return (gre, gim, weight)


def body(spectra, window_gain, dead_mask, order):
    f32 = jnp.float32
    bf16 = jnp.bfloat16
    scaled = (
        dead_mask.astype(f32)[:, :, None, None]
        * window_gain[:, None, None, None]
        * spectra.astype(f32)
    ).astype(bf16)
    sources = order.shape[0]
    per_dev = sources // lax.axis_size("chan")
    channels = spectra.shape[1]
    cells = sources * channels * lax.axis_size("chan") * spectra.shape[3]
    local = lax.all_to_all(scaled, "win", split_axis=3, concat_axis=0, tiled=True)
    first = lax.axis_index("chan") * per_dev
    mine = lax.dynamic_slice_in_dim(order, first, per_dev, 0)
    picked = jnp.take(local, mine, axis=1)
    gathered = lax.all_gather(picked, "chan", axis=1, tiled=True)
    gre, gim, weight = solve_stack(
        gathered[:, :, 0, :], gathered[:, :, 1, :], local[:, :, 0, :], local[:, :, 1, :], cells
    )
    stack = jnp.stack([gre, gim], axis=2)
    count = weight.shape[0]
    normed = weight * (count / jnp.sum(weight))
    first_window = lax.axis_index("win") * spectra.shape[0]
    window_weight = lax.dynamic_slice_in_dim(normed, first_window, spectra.shape[0], 0)
    return (stack, window_weight)


def solution(mesh):
    placed = (P("win", "chan", None, None), P("win"), P("win", "chan"), P())
    return jax.shard_map(
        body,
        mesh=mesh,
        in_specs=placed,
        out_specs=(P(None, "chan", None, "win"), P("win")),
        check_vma=False,
    )
```

profile of v0, /device:TPU:0, one launch (start us, length us, event | category | flops | bytes accessed | tf_op | source)
XLA Modules:
  0.0 486.9 jit_solution(12815705863949244203)
XLA Ops:
  25.4 8.3 %all-to-all-done = bf16[2,2,65536]{2,1,0:T(2,128)(2,1)S(1)} async-done(((bf16[2,2,65536]{2,1,0:T(2,128)(2,1)}), bf16[2,2,65536]{2,1,0:T(2,128)(2,1)S(1)}, u32[]{:S(2)}, u32[]{:S(2)}) %all-to-all-start) | async-done | bytes 524320 | tf_op jit(solution)/shard_map/all_to_all | solution.py:62
  53.3 72.2 %all-gather.2.cloned.1.call-done = bf16[8,256,2,1024]{3,0,2,1:T(8,128)(2,1)} async-done(((bf16[8,16,2,1024]{3,0,2,1:T(8,128)(2,1)}), bf16[8,256,2,1024]{3,0,2,1:T(8,128)(2,1)}) %all-gather.2.cloned.1.call-update) | async-done | bytes 8388624 | tf_op jit(solution)/shard_map/all_gather | solution.py:66
  138.8 10.1 %fusion.52 = f32[1024,16,256]{2,1,0:T(8,128)} fusion(bf16[8,256,1,1024]{1,0,3,2:T(8,128)(2,1)} %copy.28, bf16[8,16,2,1024]{1,0,3,2:T(8,128)(2,1)} %bitcast.154), kind=kOutput, calls=%fused_computation.73 | convolution fusion | flops 67108864 | bytes 23068672 | tf_op jit(solution)/shard_map/ksf,kcf->scf/dot_general | solution.py:25
  155.6 7.3 %copy.29 = bf16[8,256,1,1024]{1,0,3,2:T(8,128)(2,1)} copy(bf16[8,256,1,1024]{3,0,2,1:T(8,128)(2,1)} %get-tuple-element.13) | data formatting | bytes 8388608
  168.3 10.9 %multiply_convert_fusion.1 = bf16[1024,16,256]{2,1,0:T(8,128)(2,1)} fusion(f32[1024,16,256]{2,1,0:T(8,128)} %fusion.52, bf16[8,256,1,1024]{1,0,3,2:T(8,128)(2,1)S(1)} %copy-done.5, bf16[8,16,2,1024]{1,0,3,2:T(8,128)(2,1)} %bitcast.155), kind=kOutput, calls=%fused_computation.9 | convolution fusion | flops 79691776 | bytes 31457280 | tf_op jit(solution)/shard_map/ksf,kcf->scf/dot_general | solution.py:25
  179.2 7.7 %fusion.12 = f32[1024,16,8]{1,2,0:T(8,128)} fusion(bf16[1024,16,256]{2,1,0:T(8,128)(2,1)} %multiply_convert_fusion.1, bf16[8,256,1,1024]{1,0,3,2:T(8,128)(2,1)S(1)} %copy-done.5), kind=kOutput, calls=%fused_computation.22 | convolution fusion | flops 67108864 | bytes 13107200 | tf_op jit(solution)/shard_map/ksf,scf->kcf/dot_general | solution.py:25
  186.8 16.6 %add_reduce_fusion.1 = (f32[]{:T(128)}, bf16[1024,16,256]{2,1,0:T(8,128)(2,1)}) fusion(bf16[1024,16,256]{2,1,0:T(8,128)(2,1)} %multiply_convert_fusion.1, f32[1024,16,256]{2,1,0:T(8,128)} %fusion.49, bf16[8,256,1,1024]{1,0,3,2:T(8,128)(2,1)} %copy.29, bf16[8,16,2,1024]{1,0,3,2:T(8,128)(2,1)} %bitcast.156), kind=kOutput, calls=%fused_computation.7 | convolution fusion | flops 104857600 | bytes 39845892 | tf_op jit(solution)/shard_map/ksf,kcf->scf/dot_general | solution.py:25
  203.4 8.8 %fusion.8 = f32[1024,16,8]{1,2,0:T(8,128)} fusion(bf16[1024,16,256]{2,1,0:T(8,128)(2,1)} %get-tuple-element.19, bf16[8,256,1,1024]{1,0,3,2:T(8,128)(2,1)} %copy.28), kind=kOutput, calls=%fused_computation.18 | convolution fusion | flops 67108864 | bytes 13107200 | tf_op jit(solution)/shard_map/ksf,scf->kcf/dot_general | solution.py:25
  212.2 9.0 %fusion.10 = f32[1024,16,8]{1,2,0:T(8,128)} fusion(bf16[1024,16,256]{2,1,0:T(8,128)(2,1)} %get-tuple-element.19, bf16[8,256,1,1024]{1,0,3,2:T(8,128)(2,1)} %copy.29), kind=kOutput, calls=%fused_computation.20 | convolution fusion | flops 67108864 | bytes 13107200 | tf_op jit(solution)/shard_map/ksf,scf->kcf/dot_general | solution.py:25
  221.3 9.7 %fusion.21 = f32[8]{0:T(128)S(1)} fusion(f32[1024,16,8]{1,2,0:T(8,128)} %fusion.8, f32[1024,16,8]{1,2,0:T(8,128)} %fusion.12, f32[1024,16,8]{1,2,0:T(8,128)} %fusion.10, bf16[8,256,1,1024]{1,0,3,2:T(8,128)(2,1)S(1)} %copy-done.1, bf16[1024,16,256]{2,1,0:T(8,128)(2,1)} %multiply_convert_fusion.1, bf16[8,16,2,1024]{1,0,3,2:T(8,128)(2,1)} %bitcast.157), kind=kOutput, calls=%fused_computation.42 | convolution fusion | flops 68157432 | bytes 14680096 | tf_op jit(solution)/shard_map/ksf,scf->kcf/dot_general | solution.py:25
  231.6 38.8 %psum.14 = f32[8]{0:T(128)S(1)} all-reduce(f32[8]{0:T(128)S(1)} %subtract_add_fusion.1), channel_id=1, replica_groups=mesh['win'=2,'chan'=16] {'win','chan'}, use_global_device_ids=true, to_apply=%region_5.6 | all-reduce | flops 8 | bytes 64 | tf_op jit(solution)/shard_map/psum | solution.py:44
  271.0 10.2 %fusion.46 = f32[1024,16,256]{2,1,0:T(8,128)} fusion(bf16[8,256,1,1024]{1,0,3,2:T(8,128)(2,1)} %copy.28, f32[8]{0:T(128)S(1)} %get-tuple-element.17, bf16[8,16,2,1024]{1,0,3,2:T(8,128)(2,1)} %bitcast.158), kind=kOutput, calls=%fused_computation.67 | convolution fusion | flops 67502080 | bytes 23068704 | tf_op jit(solution)/shard_map/ksf,kcf->scf/dot_general | solution.py:25
  288.1 10.7 %divide_convert_fusion.3 = bf16[1024,16,256]{2,1,0:T(8,128)(2,1)} fusion(f32[1024,16,256]{2,1,0:T(8,128)} %fusion.46, f32[]{:T(128)} %get-tuple-element.16, bf16[8,256,1,1024]{1,0,3,2:T(8,128)(2,1)S(1)} %copy-done.6, f32[8]{0:T(128)S(1)} %get-tuple-element.17, bf16[8,16,2,1024]{1,0,3,2:T(8,128)(2,1)} %bitcast.159), kind=kOutput, calls=%fused_computation.6 | convolution fusion | flops 80084992 | bytes 31457824 | tf_op jit(solution)/shard_map/ksf,kcf->scf/dot_general | solution.py:25
  298.8 7.7 %fusion.4 = f32[1024,16,8]{1,2,0:T(8,128)} fusion(bf16[1024,16,256]{2,1,0:T(8,128)(2,1)} %divide_convert_fusion.3, bf16[8,256,1,1024]{1,0,3,2:T(8,128)(2,1)S(1)} %copy-done.6), kind=kOutput, calls=%fused_computation.14 | convolution fusion | flops 67108864 | bytes 13107200 | tf_op jit(solution)/shard_map/ksf,scf->kcf/dot_general | solution.py:25
  306.5 17.5 %add_reduce_fusion = (f32[]{:T(128)}, bf16[1024,16,256]{2,1,0:T(8,128)(2,1)}) fusion(bf16[1024,16,256]{2,1,0:T(8,128)(2,1)} %divide_convert_fusion.3, f32[]{:T(128)} %get-tuple-element.16, f32[1024,16,256]{2,1,0:T(8,128)} %fusion.43, bf16[8,256,1,1024]{1,0,3,2:T(8,128)(2,1)} %copy.29, f32[8]{0:T(128)S(1)} %get-tuple-element.17, ...), kind=kOutput, calls=%fused_computation.4 | convolution fusion | flops 105250816 | bytes 39846436 | tf_op jit(solution)/shard_map/ksf,kcf->scf/dot_general | solution.py:25
  324.0 8.8 %fusion = f32[1024,16,8]{1,2,0:T(8,128)} fusion(bf16[1024,16,256]{2,1,0:T(8,128)(2,1)} %get-tuple-element.21, bf16[8,256,1,1024]{1,0,3,2:T(8,128)(2,1)} %copy.28), kind=kOutput, calls=%fused_computation.10 | convolution fusion | flops 67108864 | bytes 13107200 | tf_op jit(solution)/shard_map/ksf,scf->kcf/dot_general | solution.py:25
  332.8 9.0 %fusion.2 = f32[1024,16,8]{1,2,0:T(8,128)} fusion(bf16[1024,16,256]{2,1,0:T(8,128)(2,1)} %get-tuple-element.21, bf16[8,256,1,1024]{1,0,3,2:T(8,128)(2,1)} %copy.29), kind=kOutput, calls=%fused_computation.12 | convolution fusion | flops 67108864 | bytes 13107200 | tf_op jit(solution)/shard_map/ksf,scf->kcf/dot_general | solution.py:25
  341.7 9.7 %fusion.24 = f32[8]{0:T(128)S(1)} fusion(f32[1024,16,8]{1,2,0:T(8,128)} %fusion, f32[1024,16,8]{1,2,0:T(8,128)} %fusion.4, f32[1024,16,8]{1,2,0:T(8,128)} %fusion.2, bf16[8,256,1,1024]{1,0,3,2:T(8,128)(2,1)S(1)} %copy-done.3, bf16[1024,16,256]{2,1,0:T(8,128)(2,1)} %divide_convert_fusion.3, bf16[8,16,2,1024]{1,0,3,2:T(8,128)(2,1)} %bitcast.161), kind=kOutput, calls=%fused_computation.45 | convolution fusion | flops 68157432 | bytes 14680096 | tf_op jit(solution)/shard_map/ksf,scf->kcf/dot_general | solution.py:25
  352.0 40.6 %psum.15 = f32[8]{0:T(128)S(1)} all-reduce(f32[8]{0:T(128)S(1)} %subtract_add_fusion), channel_id=1, replica_groups=mesh['win'=2,'chan'=16] {'win','chan'}, use_global_device_ids=true, to_apply=%region_9.10 | all-reduce | flops 8 | bytes 64 | tf_op jit(solution)/shard_map/psum | solution.py:44
  393.9 10.0 %fusion.38 = f32[1024,16,256]{2,1,0:T(8,128)} fusion(bf16[8,256,1,1024]{1,0,3,2:T(8,128)(2,1)} %copy.28, f32[8]{0:T(128)S(1)} %get-tuple-element.15, bf16[8,16,2,1024]{1,0,3,2:T(8,128)(2,1)} %bitcast.162), kind=kOutput, calls=%fused_computation.59 | convolution fusion | flops 67502080 | bytes 23068704 | tf_op jit(solution)/shard_map/ksf,kcf->scf/dot_general | solution.py:25
  410.8 11.8 %fusion.17 = bf16[256,16,1,1024]{0,1,3,2:T(8,128)(2,1)} fusion(f32[]{:T(128)} %fusion.71, f32[1024,16,256]{2,1,0:T(8,128)} %fusion.38, bf16[8,256,1,1024]{1,0,3,2:T(8,128)(2,1)S(1)} %copy-done.7, f32[8]{0:T(128)S(1)} %get-tuple-element.15, bf16[8,16,2,1024]{1,0,3,2:T(8,128)(2,1)S(1)} %bitcast.166), kind=kOutput, calls=%fused_computation.38 | convolution fusion | flops 80084992 | bytes 31457796 | tf_op jit(solution)/shard_map/ksf,kcf->scf/dot_general | solution.py:25
  422.6 11.8 %fusion.16 = bf16[256,16,1,1024]{0,1,3,2:T(8,128)(2,1)} fusion(f32[]{:T(128)} %fusion.71, f32[1024,16,256]{2,1,0:T(8,128)} %fusion.40, bf16[8,256,1,1024]{1,0,3,2:T(8,128)(2,1)S(1)} %copy-done.7, f32[8]{0:T(128)S(1)} %get-tuple-element.15, bf16[8,16,2,1024]{1,0,3,2:T(8,128)(2,1)S(1)} %bitcast.167), kind=kOutput, calls=%fused_computation.37 | convolution fusion | flops 80084992 | bytes 31457796 | tf_op jit(solution)/shard_map/ksf,kcf->scf/dot_general | solution.py:25
  434.5 13.7 %pad_maximum_fusion = bf16[256,16,2,1024]{0,1,3,2:T(8,128)(2,1)} fusion(bf16[256,16,1,1024]{0,1,3,2:T(8,128)(2,1)} %fusion.17, bf16[256,16,1,1024]{0,1,3,2:T(8,128)(2,1)} %fusion.16), kind=kLoop, calls=%fused_computation.1 | loop fusion | flops 8388608 | bytes 33554432 | tf_op jit(solution)/shard_map/stack | solution.py:70
  448.2 31.0 %copy.27 = bf16[256,16,2,1024]{3,2,1,0:T(2,128)(2,1)} copy(bf16[256,16,2,1024]{0,1,3,2:T(8,128)(2,1)} %pad_maximum_fusion) | data formatting | bytes 33554432
  (52 shorter events, 80.1 us)
Async XLA Ops:
  9.4 15.9 %copy-start.11 = (s32[256]{0:T(256)S(1)}, s32[256]{0:T(256)}, u32[]{:S(2)}) copy-start(s32[256]{0:T(256)} %param.7) | copy-start | bytes 3076
  20.8 12.9 %all-to-all-start = ((bf16[2,2,65536]{2,1,0:T(2,128)(2,1)}), bf16[2,2,65536]{2,1,0:T(2,128)(2,1)S(1)}, u32[]{:S(2)}, u32[]{:S(2)}) async-start(bf16[2,2,65536]{2,1,0:T(2,128)(2,1)} %reshape.25), calls=%async_computation | async-start | bytes 1048576 | tf_op jit(solution)/shard_map/all_to_all | solution.py:62
  25.0 100.5 %all-gather.2.cloned.1.call-start = ((), (), s32[]{:S(2)}) async-start(), calls=%async_computation.1 | async-start | bytes 8912896 | tf_op jit(solution)/shard_map/all_gather | solution.py:66
  138.8 10.1 %copy-start = (bf16[8,256,1,1024]{1,0,3,2:T(8,128)(2,1)S(1)}, bf16[8,256,1,1024]{1,0,3,2:T(8,128)(2,1)}, u32[]{:S(2)}) copy-start(bf16[8,256,1,1024]{1,0,3,2:T(8,128)(2,1)} %copy.28) | copy-start | bytes 12582916
  138.8 10.1 %copy-start.8 = (bf16[4,16,2,2,1024]{1,0,3,4,2:T(4,128)(2,1)S(1)}, bf16[4,16,2,2,1024]{1,0,3,4,2:T(4,128)(2,1)}, u32[]{:S(2)}) copy-start(bf16[4,16,2,2,1024]{1,0,3,4,2:T(4,128)(2,1)} %copy.23) | copy-start | bytes 1572868
  163.0 5.3 %copy-start.5 = (bf16[8,256,1,1024]{1,0,3,2:T(8,128)(2,1)S(1)}, bf16[8,256,1,1024]{1,0,3,2:T(8,128)(2,1)}, u32[]{:S(2)}) copy-start(bf16[8,256,1,1024]{1,0,3,2:T(8,128)(2,1)} %copy.29) | copy-start | bytes 12582916
  212.2 9.1 %copy-start.1 = (bf16[8,256,1,1024]{1,0,3,2:T(8,128)(2,1)S(1)}, bf16[8,256,1,1024]{1,0,3,2:T(8,128)(2,1)}, u32[]{:S(2)}) copy-start(bf16[8,256,1,1024]{1,0,3,2:T(8,128)(2,1)} %copy.28) | copy-start | bytes 12582916
  271.0 10.2 %copy-start.2 = (bf16[8,256,1,1024]{1,0,3,2:T(8,128)(2,1)S(1)}, bf16[8,256,1,1024]{1,0,3,2:T(8,128)(2,1)}, u32[]{:S(2)}) copy-start(bf16[8,256,1,1024]{1,0,3,2:T(8,128)(2,1)} %copy.28) | copy-start | bytes 12582916
  271.0 10.2 %copy-start.9 = (bf16[4,16,2,2,1024]{1,0,3,4,2:T(4,128)(2,1)S(1)}, bf16[4,16,2,2,1024]{1,0,3,4,2:T(4,128)(2,1)}, u32[]{:S(2)}) copy-start(bf16[4,16,2,2,1024]{1,0,3,4,2:T(4,128)(2,1)} %copy.23) | copy-start | bytes 1572868
  281.2 6.9 %copy-start.6 = (bf16[8,256,1,1024]{1,0,3,2:T(8,128)(2,1)S(1)}, bf16[8,256,1,1024]{1,0,3,2:T(8,128)(2,1)}, u32[]{:S(2)}) copy-start(bf16[8,256,1,1024]{1,0,3,2:T(8,128)(2,1)} %copy.29) | copy-start | bytes 12582916
  332.8 9.0 %copy-start.3 = (bf16[8,256,1,1024]{1,0,3,2:T(8,128)(2,1)S(1)}, bf16[8,256,1,1024]{1,0,3,2:T(8,128)(2,1)}, u32[]{:S(2)}) copy-start(bf16[8,256,1,1024]{1,0,3,2:T(8,128)(2,1)} %copy.28) | copy-start | bytes 12582916
  393.9 10.0 %copy-start.4 = (bf16[8,256,1,1024]{1,0,3,2:T(8,128)(2,1)S(1)}, bf16[8,256,1,1024]{1,0,3,2:T(8,128)(2,1)}, u32[]{:S(2)}) copy-start(bf16[8,256,1,1024]{1,0,3,2:T(8,128)(2,1)} %copy.28) | copy-start | bytes 12582916
  393.9 10.0 %copy-start.10 = (bf16[4,16,2,2,1024]{1,0,3,4,2:T(4,128)(2,1)S(1)}, bf16[4,16,2,2,1024]{1,0,3,4,2:T(4,128)(2,1)}, u32[]{:S(2)}) copy-start(bf16[4,16,2,2,1024]{1,0,3,4,2:T(4,128)(2,1)} %copy.23) | copy-start | bytes 1572868
  403.9 6.9 %copy-start.7 = (bf16[8,256,1,1024]{1,0,3,2:T(8,128)(2,1)S(1)}, bf16[8,256,1,1024]{1,0,3,2:T(8,128)(2,1)}, u32[]{:S(2)}) copy-start(bf16[8,256,1,1024]{1,0,3,2:T(8,128)(2,1)} %copy.29) | copy-start | bytes 12582916
Sparse Core Ops, SparseCore 0:
  50.0 75.4 all-gather.1
where the time goes:
time: 492 us; the launch traced here: 487 us
  matrix products  200 us (41%)
  waiting for transfers between devices  80.5 us (16%)
  blocking collectives  79.4 us (16%)
  local copies, waits for them, and re-layouts  78.8 us (16%)
  other arithmetic  28.3 us (6%)
  between operations  15.1 us (3%)
    dot_general x20, matrix products, product(): return jnp.einsum(form, left, right, preferred_element_type=f32)  200 us
    psum x2, blocking collectives, solve_stack(): misfit = lax.psum(partial_misfit, ('win', 'chan'))  79.4 us
    all_gather x1, waiting for transfers between devices, body(): gathered = lax.all_gather(picked, 'chan', axis=1, tiled=True)  72.2 us
    unnamed x29, local copies, waits for them, and re-layouts  56.4 us
    another operation x1, other arithmetic, body(): stack = jnp.stack([gre, gim], axis=2)  13.7 us
    all_to_all x2, local copies, waits for them, and re-layouts, body(): lax.all_to_all(scaled, 'win', split_axis=3, concat_axis=0, tiled=True)  10.5 us
  transfers between devices with their start and end apart: 2, of which 2 were waited for; matrix products, arithmetic and copies ran while one was open for 1% of the time, Pallas kernels for 0%

commit v1 on v0

--- a/solution.py
+++ b/solution.py
@@ -4,6 +4,27 @@
 from jax.sharding import PartitionSpec as P
 
 ITERS = 2
+
+
+def ring_gather(value, axis, dim):
+    size, here, rows = (lax.axis_size(axis), lax.axis_index(axis), value.shape[dim])
+    ahead = [(i, (i + 1) % size) for i in range(size)]
+    behind = [(i, (i - 1) % size) for i in range(size)]
+    filled = jnp.zeros((*value.shape[:dim], size * rows, *value.shape[dim + 1 :]), value.dtype)
+    filled = lax.dynamic_update_slice_in_dim(filled, value, here * rows, axis=dim)
+    from_left = from_right = value
+    half = size // 2
+    for step in range(1, half + 1):
+        from_left = lax.ppermute(from_left, axis, ahead)
+        filled = lax.dynamic_update_slice_in_dim(
+            filled, from_left, (here - step) % size * rows, axis=dim
+        )
+        if step < size - half:
+            from_right = lax.ppermute(from_right, axis, behind)
+            filled = lax.dynamic_update_slice_in_dim(
+                filled, from_right, (here + step) % size * rows, axis=dim
+            )
+    return filled
 
 
 def solve_stack(src_re, src_im, ch_re, ch_im, cells):
@@ -63,7 +84,7 @@
     first = lax.axis_index("chan") * per_dev
     mine = lax.dynamic_slice_in_dim(order, first, per_dev, 0)
     picked = jnp.take(local, mine, axis=1)
-    gathered = lax.all_gather(picked, "chan", axis=1, tiled=True)
+    gathered = ring_gather(picked, "chan", 1)
     gre, gim, weight = solve_stack(
         gathered[:, :, 0, :], gathered[:, :, 1, :], local[:, :, 0, :], local[:, :, 1, :], cells
     )

time: 492 us -> 5410 us (11.00)
  local copies, waits for them, and re-layouts: 78.8 us -> 4980 us
  starting transfers between devices: 4.49 us -> 70.5 us
    dynamic_update_slice x0 -> x16, local copies, waits for them, and re-layouts: none -> 4840 us  [the longest x8 2420 us: ring_gather(): lax.dynamic_update_slice_in_dim(filled, from_left, (here - step) % size *...]
    all_gather x1 -> x0, waiting for transfers between devices: 72.2 us -> none  [body(): gathered = lax.all_gather(picked, 'chan', axis=1, tiled=True)]
    ppermute x0 -> x15, starting transfers between devices: none -> 66.3 us  [the longest x8 59.5 us: ring_gather(): from_left = lax.ppermute(from_left, axis, ahead)]
    ppermute x0 -> x15, local copies, waits for them, and re-layouts: none -> 65.8 us  [the longest x8 34.5 us: ring_gather(): from_left = lax.ppermute(from_left, axis, ahead)]
  transfers between devices with their start and end apart: 2 -> 16, of which waited for: 2 -> 8; matrix products, arithmetic and copies ran while one was open for 1% -> 90% of each run, Pallas kernels for 0% -> 0%
where the time goes in v1:
time: 5410 us; the launch traced here: 5400 us
  local copies, waits for them, and re-layouts  4980 us (92%)
  matrix products  206 us (4%)
  blocking collectives  80.4 us (1%)
  starting transfers between devices  70.5 us (1%)
    dynamic_update_slice x8, local copies, waits for them, and re-layouts, ring_gather(): lax.dynamic_update_slice_in_dim(filled, from_left, (here - step) % size *...  2420 us
    dynamic_update_slice x7, local copies, waits for them, and re-layouts, ring_gather(): lax.dynamic_update_slice_in_dim(filled, from_right, (here + step) % size...  2360 us
    dot_general x20, matrix products, product(): return jnp.einsum(form, left, right, preferred_element_type=f32)  206 us
  transfers between devices with their start and end apart: 16, of which 8 were waited for; matrix products, arithmetic and copies ran while one was open for 90% of the time, Pallas kernels for 0%

profile of v1, /device:TPU:0, one launch (start us, length us, event | category | flops | bytes accessed | tf_op | source)
XLA Modules:
  0.0 5401.5 jit_solution(12372326176181425952)
XLA Ops:
  113.5 12.7 collective-permute-start.12
  127.8 12.7 collective-permute-start.14
  148.6 63.8 %dynamic_update_slice.48 = bf16[8,256,2,1024]{1,0,3,2:T(8,128)(2,1)} dynamic-update-slice(bf16[8,256,2,1024]{1,0,3,2:T(8,128)(2,1)} %broadcast_in_dim.19, bf16[8,16,2,1024]{1,0,3,2:T(8,128)(2,1)} %copy.68, s32[]{:T(128)} %constant.117.clone.1, s32[]{:T(128)S(6)} %select_n.124, s32[]{:T(128)} %constant.117.clone.1, s32[]{:T(128)} %constant.117.clone.1) | dynamic-update-slice | bytes 1048580 | tf_op jit(solution)/shard_map/dynamic_update_slice | solution.py:14
  220.0 336.4 %dynamic_update_slice.49 = bf16[8,256,2,1024]{1,0,3,2:T(8,128)(2,1)} dynamic-update-slice(bf16[8,256,2,1024]{1,0,3,2:T(8,128)(2,1)} %dynamic_update_slice.48, bf16[8,16,2,1024]{1,0,3,2:T(8,128)(2,1)} %copy.70, s32[]{:T(128)} %constant.117.clone.1, s32[]{:T(128)S(6)} %select_n.128, s32[]{:T(128)} %constant.117.clone.1, s32[]{:T(128)} %constant.117.clone.1) | dynamic-update-slice | bytes 1048580 | tf_op jit(solution)/shard_map/dynamic_update_slice | solution.py:19
  560.6 337.1 %dynamic_update_slice.50 = bf16[8,256,2,1024]{1,0,3,2:T(8,128)(2,1)} dynamic-update-slice(bf16[8,256,2,1024]{1,0,3,2:T(8,128)(2,1)} %dynamic_update_slice.49, bf16[8,16,2,1024]{1,0,3,2:T(8,128)(2,1)} %copy.72, s32[]{:T(128)} %constant.117.clone.1, s32[]{:T(128)S(6)} %select_n.130, s32[]{:T(128)} %constant.117.clone.1, s32[]{:T(128)} %constant.117.clone.1) | dynamic-update-slice | bytes 1048580 | tf_op jit(solution)/shard_map/dynamic_update_slice | solution.py:24
  901.8 336.5 %dynamic_update_slice.51 = bf16[8,256,2,1024]{1,0,3,2:T(8,128)(2,1)} dynamic-update-slice(bf16[8,256,2,1024]{1,0,3,2:T(8,128)(2,1)} %dynamic_update_slice.50, bf16[8,16,2,1024]{1,0,3,2:T(8,128)(2,1)} %copy.73, s32[]{:T(128)} %constant.117.clone.1, s32[]{:T(128)S(6)} %select_n.132, s32[]{:T(128)} %constant.117.clone.1, s32[]{:T(128)} %constant.117.clone.1) | dynamic-update-slice | bytes 1048580 | tf_op jit(solution)/shard_map/dynamic_update_slice | solution.py:19
  1242.4 337.1 %dynamic_update_slice.52 = bf16[8,256,2,1024]{1,0,3,2:T(8,128)(2,1)} dynamic-update-slice(bf16[8,256,2,1024]{1,0,3,2:T(8,128)(2,1)} %dynamic_update_slice.51, bf16[8,16,2,1024]{1,0,3,2:T(8,128)(2,1)} %copy.74, s32[]{:T(128)} %constant.117.clone.1, s32[]{:T(128)S(6)} %select_n.134, s32[]{:T(128)} %constant.117.clone.1, s32[]{:T(128)} %constant.117.clone.1) | dynamic-update-slice | bytes 1048580 | tf_op jit(solution)/shard_map/dynamic_update_slice | solution.py:24
  1583.6 336.5 %dynamic_update_slice.53 = bf16[8,256,2,1024]{1,0,3,2:T(8,128)(2,1)} dynamic-update-slice(bf16[8,256,2,1024]{1,0,3,2:T(8,128)(2,1)} %dynamic_update_slice.52, bf16[8,16,2,1024]{1,0,3,2:T(8,128)(2,1)} %copy.75, s32[]{:T(128)} %constant.117.clone.1, s32[]{:T(128)S(6)} %select_n.136, s32[]{:T(128)} %constant.117.clone.1, s32[]{:T(128)} %constant.117.clone.1) | dynamic-update-slice | bytes 1048580 | tf_op jit(solution)/shard_map/dynamic_update_slice | solution.py:19
  1924.2 337.1 %dynamic_update_slice.54 = bf16[8,256,2,1024]{1,0,3,2:T(8,128)(2,1)} dynamic-update-slice(bf16[8,256,2,1024]{1,0,3,2:T(8,128)(2,1)} %dynamic_update_slice.53, bf16[8,16,2,1024]{1,0,3,2:T(8,128)(2,1)} %copy.76, s32[]{:T(128)} %constant.117.clone.1, s32[]{:T(128)S(6)} %select_n.138, s32[]{:T(128)} %constant.117.clone.1, s32[]{:T(128)} %constant.117.clone.1) | dynamic-update-slice | bytes 1048580 | tf_op jit(solution)/shard_map/dynamic_update_slice | solution.py:24
  2265.8 336.5 %dynamic_update_slice.55 = bf16[8,256,2,1024]{1,0,3,2:T(8,128)(2,1)} dynamic-update-slice(bf16[8,256,2,1024]{1,0,3,2:T(8,128)(2,1)} %dynamic_update_slice.54, bf16[8,16,2,1024]{1,0,3,2:T(8,128)(2,1)} %copy.77, s32[]{:T(128)} %constant.117.clone.1, s32[]{:T(128)S(6)} %select_n.140, s32[]{:T(128)} %constant.117.clone.1, s32[]{:T(128)} %constant.117.clone.1) | dynamic-update-slice | bytes 1048580 | tf_op jit(solution)/shard_map/dynamic_update_slice | solution.py:19
  2606.5 337.1 %dynamic_update_slice.56 = bf16[8,256,2,1024]{1,0,3,2:T(8,128)(2,1)} dynamic-update-slice(bf16[8,256,2,1024]{1,0,3,2:T(8,128)(2,1)} %dynamic_update_slice.55, bf16[8,16,2,1024]{1,0,3,2:T(8,128)(2,1)} %copy.78, s32[]{:T(128)} %constant.117.clone.1, s32[]{:T(128)S(6)} %select_n.142, s32[]{:T(128)} %constant.117.clone.1, s32[]{:T(128)} %constant.117.clone.1) | dynamic-update-slice | bytes 1048580 | tf_op jit(solution)/shard_map/dynamic_update_slice | solution.py:24
  2947.7 336.5 %dynamic_update_slice.57 = bf16[8,256,2,1024]{1,0,3,2:T(8,128)(2,1)} dynamic-update-slice(bf16[8,256,2,1024]{1,0,3,2:T(8,128)(2,1)} %dynamic_update_slice.56, bf16[8,16,2,1024]{1,0,3,2:T(8,128)(2,1)} %copy.79, s32[]{:T(128)} %constant.117.clone.1, s32[]{:T(128)S(6)} %select_n.144, s32[]{:T(128)} %constant.117.clone.1, s32[]{:T(128)} %constant.117.clone.1) | dynamic-update-slice | bytes 1048580 | tf_op jit(solution)/shard_map/dynamic_update_slice | solution.py:19
  3288.3 337.1 %dynamic_update_slice.58 = bf16[8,256,2,1024]{1,0,3,2:T(8,128)(2,1)} dynamic-update-slice(bf16[8,256,2,1024]{1,0,3,2:T(8,128)(2,1)} %dynamic_update_slice.57, bf16[8,16,2,1024]{1,0,3,2:T(8,128)(2,1)} %copy.80, s32[]{:T(128)} %constant.117.clone.1, s32[]{:T(128)S(6)} %select_n.146, s32[]{:T(128)} %constant.117.clone.1, s32[]{:T(128)} %constant.117.clone.1) | dynamic-update-slice | bytes 1048580 | tf_op jit(solution)/shard_map/dynamic_update_slice | solution.py:24
  3629.5 336.4 %dynamic_update_slice.59 = bf16[8,256,2,1024]{1,0,3,2:T(8,128)(2,1)} dynamic-update-slice(bf16[8,256,2,1024]{1,0,3,2:T(8,128)(2,1)} %dynamic_update_slice.58, bf16[8,16,2,1024]{1,0,3,2:T(8,128)(2,1)} %copy.81, s32[]{:T(128)} %constant.117.clone.1, s32[]{:T(128)S(6)} %select_n.148, s32[]{:T(128)} %constant.117.clone.1, s32[]{:T(128)} %constant.117.clone.1) | dynamic-update-slice | bytes 1048580 | tf_op jit(solution)/shard_map/dynamic_update_slice | solution.py:19
  3971.3 337.1 %dynamic_update_slice.60 = bf16[8,256,2,1024]{1,0,3,2:T(8,128)(2,1)} dynamic-update-slice(bf16[8,256,2,1024]{1,0,3,2:T(8,128)(2,1)} %dynamic_update_slice.59, bf16[8,16,2,1024]{1,0,3,2:T(8,128)(2,1)} %copy.82, s32[]{:T(128)} %constant.117.clone.1, s32[]{:T(128)S(6)} %select_n.150, s32[]{:T(128)} %constant.117.clone.1, s32[]{:T(128)} %constant.117.clone.1) | dynamic-update-slice | bytes 1048580 | tf_op jit(solution)/shard_map/dynamic_update_slice | solution.py:24
  4312.5 336.4 %dynamic_update_slice.61 = bf16[8,256,2,1024]{1,0,3,2:T(8,128)(2,1)} dynamic-update-slice(bf16[8,256,2,1024]{1,0,3,2:T(8,128)(2,1)} %dynamic_update_slice.60, bf16[8,16,2,1024]{1,0,3,2:T(8,128)(2,1)} %copy.83, s32[]{:T(128)} %constant.117.clone.1, s32[]{:T(128)S(6)} %select_n.152, s32[]{:T(128)} %constant.117.clone.1, s32[]{:T(128)} %constant.117.clone.1) | dynamic-update-slice | bytes 1048580 | tf_op jit(solution)/shard_map/dynamic_update_slice | solution.py:19
  4654.2 337.1 %dynamic_update_slice.62 = bf16[8,256,2,1024]{1,0,3,2:T(8,128)(2,1)} dynamic-update-slice(bf16[8,256,2,1024]{1,0,3,2:T(8,128)(2,1)} %dynamic_update_slice.61, bf16[8,16,2,1024]{1,0,3,2:T(8,128)(2,1)} %copy.84, s32[]{:T(128)} %constant.117.clone.1, s32[]{:T(128)S(6)} %select_n.154, s32[]{:T(128)} %constant.117.clone.1, s32[]{:T(128)} %constant.117.clone.1) | dynamic-update-slice | bytes 1048580 | tf_op jit(solution)/shard_map/dynamic_update_slice | solution.py:24
  4996.6 63.0 %dynamic_update_slice.63 = bf16[8,256,2,1024]{1,0,3,2:T(8,128)(2,1)} dynamic-update-slice(bf16[8,256,2,1024]{1,0,3,2:T(8,128)(2,1)} %dynamic_update_slice.62, bf16[8,16,2,1024]{1,0,3,2:T(8,128)(2,1)} %copy.85, s32[]{:T(128)} %constant.117.clone.1, s32[]{:T(128)S(6)} %select_n.156, s32[]{:T(128)} %constant.117.clone.1, s32[]{:T(128)} %constant.117.clone.1) | dynamic-update-slice | bytes 1048580 | tf_op jit(solution)/shard_map/dynamic_update_slice | solution.py:19
  5111.4 16.7 add_reduce_fusion.1
  5147.6 40.3 psum.14
  5237.1 17.6 add_reduce_fusion
  5274.1 40.1 psum.15
  5355.8 13.7 pad_maximum_fusion
  5369.5 31.0 copy.86
  (141 shorter events, 372.9 us)
Async XLA Ops:
  14.3 12.9 all-to-all-start
  42.9 11.5 collective-permute-start
  42.9 13.6 collective-permute-start.1
  54.3 11.4 collective-permute-start.2
  56.6 13.5 collective-permute-start.3
  65.7 11.4 collective-permute-start.4
  70.0 13.5 collective-permute-start.5
  77.1 11.3 collective-permute-start.6
  83.5 14.2 collective-permute-start.7
  88.5 11.4 collective-permute-start.8
  97.7 14.2 collective-permute-start.9
  99.9 13.6 collective-permute-start.10
  111.9 14.2 collective-permute-start.11
  113.5 14.3 collective-permute-start.12
  126.1 4522.7 %collective-permute-start.13 = (bf16[8,16,2,1024]{3,1,2,0:T(8,128)(2,1)}, bf16[8,16,2,1024]{3,1,2,0:T(8,128)(2,1)}, u32[]{:S(2)}, u32[]{:S(2)}) collective-permute-start(bf16[8,16,2,1024]{3,1,2,0:T(8,128)(2,1)} %collective-permute-done.11), channel_id=1, source_target_pairs={{0,15},{1,0},{2,1},{3,2},{4,3},{5,4},{6,5},{7,6},{8,7},{9,8},{10,9... | collective-permute-start | bytes 1572872 | tf_op jit(solution)/shard_map/ppermute | solution.py:23
  127.8 4863.5 %collective-permute-start.14 = (bf16[8,16,2,1024]{3,1,2,0:T(8,128)(2,1)S(1)}, bf16[8,16,2,1024]{3,1,2,0:T(8,128)(2,1)}, u32[]{:S(2)}, u32[]{:S(2)}) collective-permute-start(bf16[8,16,2,1024]{3,1,2,0:T(8,128)(2,1)S(1)} %collective-permute-done.12), channel_id=1, source_target_pairs={{0,1},{1,2},{2,3},{3,4},{4,5},{5,6},{6,7},{7,8},{8,9},{9,10},{10,1... | collective-permute-start | bytes 1572872 | tf_op jit(solution)/shard_map/ppermute | solution.py:18
  901.8 336.5 %copy-start.9 = (bf16[8,16,2,1024]{3,1,2,0:T(8,128)(2,1)S(1)}, bf16[8,16,2,1024]{3,1,2,0:T(8,128)(2,1)}, u32[]{:S(2)}) copy-start(bf16[8,16,2,1024]{3,1,2,0:T(8,128)(2,1)} %copy-done.8) | copy-start | bytes 1572868
  1242.4 337.1 %copy-start.11 = (bf16[8,16,2,1024]{3,1,2,0:T(8,128)(2,1)S(1)}, bf16[8,16,2,1024]{3,1,2,0:T(8,128)(2,1)}, u32[]{:S(2)}) copy-start(bf16[8,16,2,1024]{3,1,2,0:T(8,128)(2,1)} %copy-done.10) | copy-start | bytes 1572868
  1583.6 336.5 %copy-start.13 = (bf16[8,16,2,1024]{3,1,2,0:T(8,128)(2,1)S(1)}, bf16[8,16,2,1024]{3,1,2,0:T(8,128)(2,1)}, u32[]{:S(2)}) copy-start(bf16[8,16,2,1024]{3,1,2,0:T(8,128)(2,1)} %copy-done.12) | copy-start | bytes 1572868
  1924.2 337.1 %copy-start.15 = (bf16[8,16,2,1024]{3,1,2,0:T(8,128)(2,1)S(1)}, bf16[8,16,2,1024]{3,1,2,0:T(8,128)(2,1)}, u32[]{:S(2)}) copy-start(bf16[8,16,2,1024]{3,1,2,0:T(8,128)(2,1)} %copy-done.14) | copy-start | bytes 1572868
  2265.8 336.5 %copy-start.17 = (bf16[8,16,2,1024]{3,1,2,0:T(8,128)(2,1)S(1)}, bf16[8,16,2,1024]{3,1,2,0:T(8,128)(2,1)}, u32[]{:S(2)}) copy-start(bf16[8,16,2,1024]{3,1,2,0:T(8,128)(2,1)} %copy-done.16) | copy-start | bytes 1572868
  2606.5 337.1 %copy-start.19 = (bf16[8,16,2,1024]{3,1,2,0:T(8,128)(2,1)S(1)}, bf16[8,16,2,1024]{3,1,2,0:T(8,128)(2,1)}, u32[]{:S(2)}) copy-start(bf16[8,16,2,1024]{3,1,2,0:T(8,128)(2,1)} %copy-done.18) | copy-start | bytes 1572868
  2947.7 336.5 %copy-start.21 = (bf16[8,16,2,1024]{3,1,2,0:T(8,128)(2,1)S(1)}, bf16[8,16,2,1024]{3,1,2,0:T(8,128)(2,1)}, u32[]{:S(2)}) copy-start(bf16[8,16,2,1024]{3,1,2,0:T(8,128)(2,1)} %copy-done.20) | copy-start | bytes 1572868
  3288.3 337.1 %copy-start.23 = (bf16[8,16,2,1024]{3,1,2,0:T(8,128)(2,1)S(1)}, bf16[8,16,2,1024]{3,1,2,0:T(8,128)(2,1)}, u32[]{:S(2)}) copy-start(bf16[8,16,2,1024]{3,1,2,0:T(8,128)(2,1)} %copy-done.22) | copy-start | bytes 1572868
  (19 other events, 457.5 us)
